TPU v7x, 256 devices: a whole 4x4x8 slice. The times are simulated.
256 devices in a mesh: rep: 16 (over z, y_hi), section: 4 (over y_lo, core), head: 4 (over x).
Axes of the slice: x: 4, y: 4 (y_hi: 2, y_lo: 2; y = y_hi * 2 + y_lo), z: 8, core: 2. Of those that a mesh axis runs over, the one named last changes fastest.
Arguments:
- prompt_pages: bfloat16 [16, 4, 16, 16, 2, 6144], P('rep', 'section', 'head'), may hold values from -6 to 6
- page_scales: bfloat16 [16, 4, 16, 2, 48], P('rep', 'section', 'head'), may hold values from 0.099609375 to 1.5
- page_table: int32 [16, 16], P('rep'), may hold values from 0 to 15, each once within a row
- lengths: int32 [16, 8], replicated, may hold values from 1 to 32, 160 in all within a row
- route: int32 [16, 8], replicated, may hold values from 0 to 15, as said below
- queries: bfloat16 [16, 4, 16, 2, 8, 6144], P('rep', None, None, None, None, ('section', 'head')), may hold values from -6 to 6
- new_kv: bfloat16 [16, 4, 16, 2, 8, 2, 6144], P('rep', None, None, None, None, None, ('section', 'head')), may hold values from -6 to 6
Outputs:
- decode_cache: bfloat16 [16, 4, 16, 2, 32, 2, 6144], P('rep', None, None, None, None, None, ('section', 'head'))
- decode_scales: bfloat16 [16, 4, 16, 2, 2, 2, 48], P('rep', None, None, None, None, None, ('section', 'head'))
- attention: bfloat16 [16, 4, 16, 2, 8, 6144], P('rep', None, None, None, None, ('section', 'head'))
Inputs may be any that keep to these rules, and one draw needn't show every extreme that they name: `page_table`: each row is a permutation of one instance's 16 page slots; page j of request q is entry q * 2 + j. `lengths`: each row sums to 160 and holds one length 32. `route`: no replica gets more than 2 requests of one instance, and in every draw one replica gets exactly 2 from every instance.
All inputs are finite; a program needn't handle non-finite values.
Results may differ from a plain program's by a relative error of at most 0.0049.
Values may be sent and summed in bfloat16 or wider, within the bound.
A program may use at most 128 MiB of HBM per device.

v0:
```python
import math

import jax
import jax.numpy as jnp
from jax import lax
from jax.sharding import PartitionSpec as P


def slot_ranks(route):
    req_ids = jnp.arange(route.shape[1], dtype=jnp.int32)
    same_dest = route[:, :, None] == route[:, None, :]
    earlier = req_ids[None, :] < req_ids[:, None]
    return jnp.sum((same_dest & earlier[None]).astype(jnp.int32), axis=2)


def body(prompt_pages, page_scales, page_table, lengths, route, queries, new_kv):
    rep_count = lax.axis_size("rep")
    section_count = lax.axis_size("section")
    head_count = lax.axis_size("head")
    replica = lax.axis_index("rep")
    layers_here = prompt_pages.shape[1]
    pages_here = prompt_pages.shape[2]
    page_rows = prompt_pages.shape[3]
    feature_count = prompt_pages.shape[5]
    heads_total = page_scales.shape[4]
    head_dim = feature_count // heads_total
    group_count = section_count * head_count
    feat_here = feature_count // group_count
    heads_here = heads_total // group_count
    req_count = route.shape[1]
    capacity = max(2, req_count // rep_count)
    pages_each = page_table.shape[1] // req_count
    layer_count = layers_here * section_count
    span_max = page_rows * pages_each
    steps_count = queries.shape[4]
    req_ids = jnp.arange(req_count, dtype=jnp.int32)
    dest_ids = jnp.arange(rep_count, dtype=jnp.int32)
    cap_ids = jnp.arange(capacity, dtype=jnp.int32)
    page_ids = jnp.arange(pages_each, dtype=jnp.int32)
    slot_rank = slot_ranks(route)
    own_route = lax.dynamic_index_in_dim(route, replica, 0, keepdims=False)
    own_rank = lax.dynamic_index_in_dim(slot_rank, replica, 0, keepdims=False)
    send_match = (own_route[None, None, :] == dest_ids[:, None, None]) & (
        own_rank[None, None, :] == cap_ids[None, :, None]
    )
    send_live = jnp.any(send_match, axis=2)
    send_request = jnp.sum(jnp.where(send_match, req_ids[None, None, :], 0), axis=2)
    physical = page_table[0][send_request[:, :, None] * pages_each + page_ids[None, None, :]]
    recv_match = (route[:, None, :] == replica) & (slot_rank[:, None, :] == cap_ids[None, :, None])
    recv_live = jnp.any(recv_match, axis=2)
    slot_span = jnp.sum(jnp.where(recv_match, lengths[:, None, :], 0), axis=2)
    page_view = prompt_pages[0].reshape(
        layers_here, pages_here, page_rows, 2, section_count, head_count, feat_here
    )
    scale_view = page_scales[0].reshape(
        layers_here, pages_here, 1, 2, section_count, head_count, heads_here
    )
    zero_page = jnp.zeros((), prompt_pages.dtype)
    zero_scale = jnp.zeros((), page_scales.dtype)
    regrouped = (
        lax.all_to_all(
            lax.all_to_all(page_view, "section", split_axis=4, concat_axis=0, tiled=True),
            "head",
            split_axis=5,
            concat_axis=1,
            tiled=True,
        ),
        lax.all_to_all(
            lax.all_to_all(scale_view, "section", split_axis=4, concat_axis=0, tiled=True),
            "head",
            split_axis=5,
            concat_axis=1,
            tiled=True,
        ),
    )
    all_pages = regrouped[0].reshape(layer_count, pages_here * head_count, page_rows, 2, feat_here)
    all_scales = regrouped[1].reshape(layer_count, pages_here * head_count, 1, 2, heads_here)
    live_mask = send_live[None, :, :, None, None, None, None]
    slot_pages = jnp.where(live_mask, all_pages[:, physical], zero_page)
    slot_scales = jnp.where(live_mask, all_scales[:, physical], zero_scale)
    received = (
        lax.all_to_all(slot_pages, "rep", split_axis=1, concat_axis=1, tiled=True),
        lax.all_to_all(slot_scales, "rep", split_axis=1, concat_axis=1, tiled=True),
    )
    page_cache = received[0].reshape(layer_count, rep_count, capacity, span_max, 2, feat_here)
    scale_cache = received[1].reshape(layer_count, rep_count, capacity, pages_each, 2, heads_here)
    prompt_keys = page_cache[:, :, :, :, 0, :].reshape(
        layer_count, rep_count, capacity, span_max, heads_here, head_dim
    )
    prompt_values = page_cache[:, :, :, :, 1, :].reshape(
        layer_count, rep_count, capacity, span_max, heads_here, head_dim
    )
    query_rows = queries[0].reshape(
        layer_count, rep_count, capacity, steps_count, heads_here, head_dim
    )
    new_keys = new_kv[0][:, :, :, :, 0, :].reshape(
        layer_count, rep_count, capacity, steps_count, heads_here, head_dim
    )
    new_values = new_kv[0][:, :, :, :, 1, :].reshape(
        layer_count, rep_count, capacity, steps_count, heads_here, head_dim
    )
    score_root = math.sqrt(head_dim)
    key_scale = jnp.transpose(scale_cache[:, :, :, :, 0, :], (0, 1, 2, 4, 3))
    value_scale = jnp.transpose(scale_cache[:, :, :, :, 1, :], (0, 1, 2, 4, 3))
    prompt_dots = jnp.einsum(
        "lrcthd,lrckhd->lrchtk", query_rows, prompt_keys, preferred_element_type=jnp.float32
    )
    prompt_dots = prompt_dots.reshape(
        layer_count, rep_count, capacity, heads_here, steps_count, pages_each, page_rows
    )
    prompt_score = (
        prompt_dots * key_scale[:, :, :, :, None, :, None].astype(jnp.float32) / score_root
    )
    prompt_score = prompt_score.reshape(
        layer_count, rep_count, capacity, heads_here, steps_count, span_max
    )
    fresh_score = (
        jnp.einsum(
            "lrcthd,lrcuhd->lrchtu", query_rows, new_keys, preferred_element_type=jnp.float32
        )
        / score_root
    )
    visible = (jnp.arange(span_max, dtype=jnp.int32)[None, None, :] < slot_span[:, :, None])[
        None, :, :, None, None, :
    ]
    causal = (
        jnp.arange(steps_count, dtype=jnp.int32)[None, :]
        <= jnp.arange(steps_count, dtype=jnp.int32)[:, None]
    )
    row_max = jnp.maximum(
        jnp.max(jnp.where(visible, prompt_score, -jnp.inf), axis=-1, keepdims=True),
        jnp.max(jnp.where(causal, fresh_score, -jnp.inf), axis=-1, keepdims=True),
    )
    exp_prompt = jnp.where(visible, jnp.exp(prompt_score - row_max), 0.0)
    exp_fresh = jnp.where(causal, jnp.exp(fresh_score - row_max), 0.0)
    row_total = jnp.sum(exp_prompt, axis=-1, keepdims=True) + jnp.sum(
        exp_fresh, axis=-1, keepdims=True
    )
    value_weight = jnp.broadcast_to(
        value_scale[:, :, :, :, :, None], value_scale.shape + (page_rows,)
    )
    value_weight = value_weight.reshape(layer_count, rep_count, capacity, heads_here, span_max)[
        :, :, :, :, None, :
    ]
    prompt_weight = (exp_prompt * value_weight.astype(jnp.float32) / row_total).astype(jnp.bfloat16)
    fresh_weight = (exp_fresh / row_total).astype(jnp.bfloat16)
    attended = jnp.einsum(
        "lrchtk,lrckhd->lrcthd", prompt_weight, prompt_values, preferred_element_type=jnp.float32
    )
    attended = attended + jnp.einsum(
        "lrchtu,lrcuhd->lrcthd", fresh_weight, new_values, preferred_element_type=jnp.float32
    )
    attended = jnp.where(recv_live[None, :, :, None, None, None], attended, 0.0).astype(
        jnp.bfloat16
    )
    return (
        page_cache.reshape(1, layer_count, rep_count, capacity, span_max, 2, feat_here),
        scale_cache.reshape(1, layer_count, rep_count, capacity, pages_each, 2, heads_here),
        attended.reshape(1, layer_count, rep_count, capacity, steps_count, feat_here),
    )


def solution(mesh):
    return jax.shard_map(
        body,
        mesh=mesh,
        in_specs=(
            P("rep", "section", "head", None, None, None),
            P("rep", "section", "head", None, None),
            P("rep", None),
            P(),
            P(),
            P("rep", None, None, None, None, ("section", "head")),
            P("rep", None, None, None, None, None, ("section", "head")),
        ),
        out_specs=(
            P("rep", None, None, None, None, None, ("section", "head")),
            P("rep", None, None, None, None, None, ("section", "head")),
            P("rep", None, None, None, None, ("section", "head")),
        ),
        check_vma=False,
    )
```

profile of v0, /device:TPU:2, one launch (start us, length us, event | category | flops | bytes accessed | tf_op | source)
XLA Modules:
  0.0 288.6 jit_solution(1211873825814646515)
XLA Ops:
  0.6 0.8 reshape_squeeze.22
  1.5 0.9 copy.150
  2.4 3.3 %all-to-all-start.3 = ((bf16[1,4,1,2,4,4,3]{5,1,6,3,2,0,4:T(4,128)(2,1)}), bf16[1,4,1,2,4,4,3]{5,1,6,3,2,0,4:T(4,128)(2,1)S(1)}, u32[]{:S(2)}, u32[]{:S(2)}) async-start(bf16[1,4,1,2,4,4,3]{5,1,6,3,2,0,4:T(4,128)(2,1)} %copy.150), calls=%async_computation.3 | async-start | bytes 49152 | tf_op jit(solution)/shard_map/all_to_all | solution.py:69
  5.7 4.4 %reshape.208 = bf16[1,4,16,2,4,4,384]{6,5,4,3,2,1,0:T(4,128)(2,1)S(1)} reshape(bf16[1,1,4,16,2,6144]{5,4,3,2,1,0:T(2,128)(2,1)} %param.7) | data formatting | bytes 3145728 | tf_op jit(solution)/shard_map/reshape;squeeze | solution.py:52
  10.1 2.0 copy.144
  12.1 3.7 %all-to-all-start = ((bf16[1,4,16,2,4,4,384]{6,5,2,3,1,0,4:T(4,128)(2,1)}), bf16[1,4,16,2,4,4,384]{6,5,2,3,1,0,4:T(4,128)(2,1)S(1)}, u32[]{:S(2)}, u32[]{:S(2)}) async-start(bf16[1,4,16,2,4,4,384]{6,5,2,3,1,0,4:T(4,128)(2,1)} %copy.144), calls=%async_computation | async-start | bytes 3145728 | tf_op jit(solution)/shard_map/all_to_all | solution.py:62
  15.8 0.1 convert_reduce_fusion
  15.9 0.2 dynamic-slice_reduce_fusion
  16.1 0.1 iota_compare_fusion.4
  16.2 0.9 copy.151
  17.1 18.7 %all-to-all-done = bf16[1,4,16,2,4,4,384]{6,5,2,3,1,0,4:T(4,128)(2,1)S(1)} async-done(((bf16[1,4,16,2,4,4,384]{6,5,2,3,1,0,4:T(4,128)(2,1)}), bf16[1,4,16,2,4,4,384]{6,5,2,3,1,0,4:T(4,128)(2,1)S(1)}, u32[]{:S(2)}, u32[]{:S(2)}) %all-to-all-start) | async-done | bytes 1572896 | tf_op jit(solution)/shard_map/all_to_all | solution.py:62
  35.8 5.5 %all-to-all-start.4 = ((bf16[4,4,1,2,1,4,3]{1,0,6,4,3,2,5:T(4,128)(2,1)}), bf16[4,4,1,2,1,4,3]{1,0,6,4,3,2,5:T(4,128)(2,1)S(1)}, u32[]{:S(2)}, u32[]{:S(2)}) async-start(bf16[4,4,1,2,1,4,3]{1,0,6,4,3,2,5:T(4,128)(2,1)} %copy.151), calls=%async_computation.4 | async-start | bytes 49152 | tf_op jit(solution)/shard_map/all_to_all | solution.py:68
  41.3 0.1 fusion.24
  41.4 2.4 copy.145
  43.9 1.4 all-to-all-done.4
  45.3 5.0 %all-to-all-start.1 = ((bf16[4,4,16,2,1,4,384]{6,0,2,3,1,4,5:T(4,128)(2,1)}), bf16[4,4,16,2,1,4,384]{6,0,2,3,1,4,5:T(4,128)(2,1)S(1)}, u32[]{:S(2)}, u32[]{:S(2)}) async-start(bf16[4,4,16,2,1,4,384]{6,0,2,3,1,4,5:T(4,128)(2,1)} %copy.145), calls=%async_computation.1 | async-start | bytes 3145728 | tf_op jit(solution)/shard_map/all_to_all | solution.py:61
  50.3 0.1 copy.147
  50.4 0.1 compare_select_fusion.1
  50.5 0.1 reshape.179
  50.6 0.8 gather_fusion
  51.4 0.1 gather.12
  51.5 0.1 reshape.187
  51.6 0.1 and_reduce_fusion
  51.7 0.1 copy.142
  51.8 0.3 copy.172
  52.1 0.8 gather_fusion.2
  52.9 0.2 broadcast_select_fusion
  53.1 0.7 copy.155
  53.8 14.7 %all-to-all-done.1 = bf16[4,4,16,2,1,4,384]{6,0,2,3,1,4,5:T(4,128)(2,1)S(1)} async-done(((bf16[4,4,16,2,1,4,384]{6,0,2,3,1,4,5:T(4,128)(2,1)}), bf16[4,4,16,2,1,4,384]{6,0,2,3,1,4,5:T(4,128)(2,1)S(1)}, u32[]{:S(2)}, u32[]{:S(2)}) %all-to-all-start.1) | async-done | bytes 1572896 | tf_op jit(solution)/shard_map/all_to_all | solution.py:61
  68.5 1.1 copy-done.2
  69.6 10.2 %all-to-all-start.5 = ((bf16[4,16,2,2,1,2,3]{0,3,2,6,5,4,1:T(2,128)(2,1)}), bf16[4,16,2,2,1,2,3]{0,3,2,6,5,4,1:T(2,128)(2,1)S(1)}, u32[]{:S(2)}, u32[]{:S(2)}) async-start(bf16[4,16,2,2,1,2,3]{0,3,2,6,5,4,1:T(2,128)(2,1)} %copy.155), calls=%async_computation.5 | async-start | bytes 196608 | tf_op jit(solution)/shard_map/all_to_all | solution.py:83
  79.9 1.7 copy.146
  81.6 4.1 %gather_fusion.1 = bf16[64,4,16,2,384]{4,2,3,1,0:T(8,128)(2,1)} fusion(bf16[4,16,16,2,384]{4,2,3,1,0:T(8,128)(2,1)S(1)} %bitcast.105, s32[1024]{0:T(1024)S(1)} %pad_clamp_fusion), kind=kCustom, calls=%fused_computation.1 | custom fusion | bytes 12583168 | tf_op jit(solution)/shard_map/gather | solution.py:79
  85.7 6.1 %select_bitcast_fusion = bf16[4,16,2,2,16,2,384]{6,4,5,0,3,2,1:T(8,128)(2,1)} fusion(bf16[16,2,2,4,16,2,384]{6,4,5,3,2,1,0:T(8,128)(2,1)} %bitcast.107, pred[16,2]{1,0:T(8,128)(4,1)S(1)} %copy.142), kind=kLoop, calls=%fused_computation.3 | loop fusion | flops 3145728 | bytes 12582944 | tf_op jit(solution)/shard_map/jit(_where)/select_n | solution.py:79
  91.9 9.8 %all-to-all-start.2 = ((bf16[4,16,2,2,16,2,384]{6,4,5,0,3,2,1:T(8,128)(2,1)}), bf16[4,16,2,2,16,2,384]{6,4,5,0,3,2,1:T(8,128)(2,1)}, u32[]{:S(2)}, u32[]{:S(2)}) async-start(bf16[4,16,2,2,16,2,384]{6,4,5,0,3,2,1:T(8,128)(2,1)} %select_bitcast_fusion), calls=%async_computation.2 | async-start | bytes 12582912 | tf_op jit(solution)/shard_map/all_to_all | solution.py:82
  101.7 0.1 copy.158
  101.8 1.4 copy.183
  103.2 0.1 copy.156
  103.3 0.1 iota_compare_fusion
  103.4 2.0 select_reduce_fusion
  105.4 0.8 copy.168
  106.2 0.2 copy.160
  106.5 0.2 copy.161
  106.7 0.5 mul.35
  107.2 0.2 mul.36
  107.4 0.8 copy.162
  108.2 0.2 copy.164
  108.4 0.5 broadcast_in_dim.143
  108.9 0.2 convert_element_type.47
  109.1 0.1 copy.165
  109.2 133.8 %all-to-all-done.2 = bf16[4,16,2,2,16,2,384]{6,4,5,0,3,2,1:T(8,128)(2,1)} async-done(((bf16[4,16,2,2,16,2,384]{6,4,5,0,3,2,1:T(8,128)(2,1)}), bf16[4,16,2,2,16,2,384]{6,4,5,0,3,2,1:T(8,128)(2,1)}, u32[]{:S(2)}, u32[]{:S(2)}) %all-to-all-start.2) | async-done | bytes 6291488 | tf_op jit(solution)/shard_map/all_to_all | solution.py:82
  243.0 4.0 %copy.157 = bf16[4,16,2,2,16,2,384]{6,4,3,2,1,0,5:T(8,128)(2,1)S(1)} copy(bf16[4,16,2,2,16,2,384]{6,4,5,0,3,2,1:T(8,128)(2,1)} %all-to-all-done.2) | data formatting | bytes 12582912 | tf_op jit(solution)/shard_map/all_to_all | solution.py:82
  247.0 3.6 %fusion.29 = (bf16[4,16,2,32,1,384]{5,3,2,1,0,4:T(8,128)(2,1)}, bf16[4,16,2,32,1,384]{5,3,2,1,0,4:T(8,128)(2,1)}) fusion(bf16[4,16,2,32,2,384]{5,3,2,1,0,4:T(8,128)(2,1)S(1)} %bitcast.106), kind=kLoop, calls=%fused_computation.66 | loop fusion | bytes 12582912 | tf_op jit(solution)/shard_map/slice | solution.py:87
  250.6 9.0 %reshape_squeeze.23 = bf16[4,16,2,32,3,128]{5,4,3,2,1,0:T(4,128)(2,1)} reshape(bf16[4,16,2,32,1,384]{5,3,2,1,0,4:T(8,128)(2,1)} %get-tuple-element.22) | data formatting | bytes 6291456 | tf_op jit(solution)/shard_map/reshape;squeeze | solution.py:90
  259.6 9.0 %reshape_squeeze.24 = bf16[4,16,2,32,3,128]{5,4,3,2,1,0:T(4,128)(2,1)} reshape(bf16[4,16,2,32,1,384]{5,3,2,1,0,4:T(8,128)(2,1)} %get-tuple-element.21) | data formatting | bytes 6291456 | tf_op jit(solution)/shard_map/reshape;squeeze | solution.py:87
  268.6 4.1 %select_reduce_fusion.1 = (f32[4,16,2,3,8]{4,3,2,1,0:T(4,128)S(1)}, f32[4,16,2,3,32,8]{4,5,3,2,1,0:T(8,128)S(1)}) fusion(pred[16,2,32]{2,1,0:T(4,128)(4,1)S(1)} %iota_compare_fusion, f32[4,16,2,3,32]{4,3,2,1,0:T(4,128)} %copy.162, bf16[1,4,16,2,8,384]{5,4,3,2,1,0:T(8,128)(2,1)S(1)} %copy-done, bf16[4,16,2,32,3,128]{5,4,3,2,1,0:T(4,128)(2,1)} %reshape_squeeze.24), kind=kOutput, calls=%fused_computation.20 | convolution fusion | flops 25555968 | bytes 4387840 | tf_op jit(solution)/shard_map/lrcthd,lrckhd->lrchtk/dot_general | solution.py:105
  272.7 0.1 max.8
  272.8 1.0 bitcast_reduce_fusion
  273.8 0.7 fusion.11
  274.6 0.1 add.63
  274.6 0.3 copy-done.3
  275.0 1.6 fusion
  276.6 1.8 fusion.10
  278.4 10.2 %copy.148 = bf16[4,16,2,2,16,2,384]{6,5,4,3,2,1,0:T(2,128)(2,1)} copy(bf16[4,16,2,2,16,2,384]{6,4,5,0,3,2,1:T(8,128)(2,1)} %all-to-all-done.2) | data formatting | bytes 12582912 | tf_op jit(solution)/shard_map/all_to_all | solution.py:82
  (28 shorter events, 0.2 us)
Async XLA Ops:
  0.6 102.8 %copy-start = (bf16[1,4,16,2,8,384]{5,4,3,2,1,0:T(8,128)(2,1)S(1)}, bf16[1,4,16,2,8,384]{5,4,3,2,1,0:T(8,128)(2,1)}, u32[]{:S(2)}) copy-start(bf16[1,4,16,2,8,384]{5,4,3,2,1,0:T(8,128)(2,1)} %param.12) | copy-start | bytes 2359300
  2.4 9.7 %all-to-all-start.3 = ((bf16[1,4,1,2,4,4,3]{5,1,6,3,2,0,4:T(4,128)(2,1)}), bf16[1,4,1,2,4,4,3]{5,1,6,3,2,0,4:T(4,128)(2,1)S(1)}, u32[]{:S(2)}, u32[]{:S(2)}) async-start(bf16[1,4,1,2,4,4,3]{5,1,6,3,2,0,4:T(4,128)(2,1)} %copy.150), calls=%async_computation.3 | async-start | bytes 49152 | tf_op jit(solution)/shard_map/all_to_all | solution.py:69
  12.1 3.7 %copy-start.6 = (s32[16,8]{0,1:T(8,128)S(1)}, s32[16,8]{0,1:T(8,128)}, u32[]{:S(2)}) copy-start(s32[16,8]{0,1:T(8,128)} %param.11) | copy-start | bytes 1540
  12.1 23.8 %all-to-all-start = ((bf16[1,4,16,2,4,4,384]{6,5,2,3,1,0,4:T(4,128)(2,1)}), bf16[1,4,16,2,4,4,384]{6,5,2,3,1,0,4:T(4,128)(2,1)S(1)}, u32[]{:S(2)}, u32[]{:S(2)}) async-start(bf16[1,4,16,2,4,4,384]{6,5,2,3,1,0,4:T(4,128)(2,1)} %copy.144), calls=%async_computation | async-start | bytes 3145728 | tf_op jit(solution)/shard_map/all_to_all | solution.py:62
  35.8 9.4 %all-to-all-start.4 = ((bf16[4,4,1,2,1,4,3]{1,0,6,4,3,2,5:T(4,128)(2,1)}), bf16[4,4,1,2,1,4,3]{1,0,6,4,3,2,5:T(4,128)(2,1)S(1)}, u32[]{:S(2)}, u32[]{:S(2)}) async-start(bf16[4,4,1,2,1,4,3]{1,0,6,4,3,2,5:T(4,128)(2,1)} %copy.151), calls=%async_computation.4 | async-start | bytes 49152 | tf_op jit(solution)/shard_map/all_to_all | solution.py:68
  43.9 6.7 %copy-start.1 = (s32[1,16]{1,0:T(1,128)S(1)}, s32[1,16]{1,0:T(1,128)}, u32[]{:S(2)}) copy-start(s32[1,16]{1,0:T(1,128)} %param.9) | copy-start | bytes 196
  45.3 23.2 %all-to-all-start.1 = ((bf16[4,4,16,2,1,4,384]{6,0,2,3,1,4,5:T(4,128)(2,1)}), bf16[4,4,16,2,1,4,384]{6,0,2,3,1,4,5:T(4,128)(2,1)S(1)}, u32[]{:S(2)}, u32[]{:S(2)}) async-start(bf16[4,4,16,2,1,4,384]{6,0,2,3,1,4,5:T(4,128)(2,1)} %copy.145), calls=%async_computation.1 | async-start | bytes 3145728 | tf_op jit(solution)/shard_map/all_to_all | solution.py:61
  68.5 1.1 copy-start.2
  69.6 22.2 %all-to-all-start.5 = ((bf16[4,16,2,2,1,2,3]{0,3,2,6,5,4,1:T(2,128)(2,1)}), bf16[4,16,2,2,1,2,3]{0,3,2,6,5,4,1:T(2,128)(2,1)S(1)}, u32[]{:S(2)}, u32[]{:S(2)}) async-start(bf16[4,16,2,2,1,2,3]{0,3,2,6,5,4,1:T(2,128)(2,1)} %copy.155), calls=%async_computation.5 | async-start | bytes 196608 | tf_op jit(solution)/shard_map/all_to_all | solution.py:83
  91.8 9.8 %copy-start.7 = (s32[16,8]{0,1:T(8,128)S(1)}, s32[16,8]{0,1:T(8,128)}, u32[]{:S(2)}) copy-start(s32[16,8]{0,1:T(8,128)} %param.10) | copy-start | bytes 1540
  91.8 10.0 %copy-start.5 = (bf16[1,4,16,2,8,2,384]{6,5,4,3,2,1,0:T(2,128)(2,1)S(1)}, bf16[1,4,16,2,8,2,384]{6,5,4,3,2,1,0:T(2,128)(2,1)}, u32[]{:S(2)}) copy-start(bf16[1,4,16,2,8,2,384]{6,5,4,3,2,1,0:T(2,128)(2,1)} %param.13) | copy-start | bytes 4718596
  91.9 151.2 %all-to-all-start.2 = ((bf16[4,16,2,2,16,2,384]{6,4,5,0,3,2,1:T(8,128)(2,1)}), bf16[4,16,2,2,16,2,384]{6,4,5,0,3,2,1:T(8,128)(2,1)}, u32[]{:S(2)}, u32[]{:S(2)}) async-start(bf16[4,16,2,2,16,2,384]{6,4,5,0,3,2,1:T(8,128)(2,1)} %select_bitcast_fusion), calls=%async_computation.2 | async-start | bytes 12582912 | tf_op jit(solution)/shard_map/all_to_all | solution.py:82
  272.8 2.2 copy-start.3
  275.0 1.6 copy-start.4
where the time goes:
time: 290 us; the launch traced here: 289 us
  waiting for transfers between devices  169 us (58%)
  local copies, waits for them, and re-layouts  63.2 us (22%)
  starting transfers between devices  37.5 us (13%)
  matrix products  9.44 us (3%)
  other arithmetic  8.86 us (3%)
    all_to_all x1, waiting for transfers between devices, body(): lax.all_to_all(slot_pages, 'rep', split_axis=1, concat_axis=1, tiled=True)  134 us
    all_to_all x1, waiting for transfers between devices, body(): lax.all_to_all(page_view, 'section', split_axis=4, concat_axis=0, tiled=T...  18.7 us
    all_to_all x1, waiting for transfers between devices, body(): lax.all_to_all(lax.all_to_all(page_view, 'section', split_axis=4, concat_...  14.7 us
    all_to_all x2, local copies, waits for them, and re-layouts, body(): lax.all_to_all(slot_pages, 'rep', split_axis=1, concat_axis=1, tiled=True)  14.2 us
    all_to_all x1, starting transfers between devices, body(): lax.all_to_all(slot_scales, 'rep', split_axis=1, concat_axis=1, tiled=True)  10.2 us
    all_to_all x1, starting transfers between devices, body(): lax.all_to_all(slot_pages, 'rep', split_axis=1, concat_axis=1, tiled=True)  9.81 us
    another operation x1, local copies, waits for them, and re-layouts, body(): page_cache[:, :, :, :, 0, :]  9 us
    another operation x1, local copies, waits for them, and re-layouts, body(): page_cache[:, :, :, :, 1, :]  8.99 us
  transfers between devices with their start and end apart: 6, of which 4 were waited for; matrix products, arithmetic and copies ran while one was open for 11% of the time, Pallas kernels for 0%

commit v1 on v0

--- a/solution.py
+++ b/solution.py
@@ -2,8 +2,416 @@
 
 import jax
 import jax.numpy as jnp
+import numpy as np
 from jax import lax
+from jax.experimental import pallas as pl
+from jax.experimental.pallas import tpu as pltpu
 from jax.sharding import PartitionSpec as P
+
+MESH = pl.DeviceIdType.MESH
+NODES = 16
+RING = NODES // 2
+PORTS = 3
+ROUNDS = 16
+PARTS = 4
+REQS = 8
+STORE = REQS + PORTS * ROUNDS
+
+ROUTES = (
+    0o5555555222222210, 0o5555555222222201, 0o4645121222121045, 0o5555212221210154,
+    0o4612132222104545, 0o5531222222015554, 0o2212122210555646, 0o3121222101545455,
+    0o1313121055555512, 0o2222210155555451, 0o1312105545565515, 0o2222015455555521,
+    0o1310554545561212, 0o2201555555542221, 0o1055555555121212, 0o0155555454222222,
+    0o5555552522222210, 0o5555552522222201, 0o5546222322221045, 0o5555522122220154,
+    0o4526221222105645, 0o2122312131015554, 0o4323221310464555, 0o2232312101646565,
+    0o2222231045454555, 0o3122220155646521, 0o2222105556454623, 0o3131015555542231,
+    0o2210455656452312, 0o2101555564555232, 0o1045455546131312, 0o0154546565312122,
+)
+
+
+def links_of(source, dest, code):
+    if code == 0:
+        return []
+    z, y = divmod(source, 2)
+    step, mode = (1, (code - 1) % 3) if code <= 3 else (-1, (code - 1) % 3)
+    cross = y != dest % 2
+    hops = [2] if (cross and mode == 0) or (not cross and mode == 2) else []
+    hops += [0 if step > 0 else 1] * (((dest // 2 - z) * step) % RING)
+    if (cross and mode != 0) or (not cross and mode == 2):
+        hops += [2]
+    links = []
+    for port in hops:
+        links.append((z * 2 + y) * PORTS + port)
+        if port == 2:
+            y = 1 - y
+        else:
+            z = (z + (1 if port == 0 else -1)) % RING
+    assert z * 2 + y == dest and len(links) < 8
+    return links
+
+
+def path_table():
+    table = np.zeros((2, NODES, 8, NODES), np.float32)
+    for rank in range(2):
+        for source in range(NODES):
+            for dest in range(NODES):
+                code = (ROUTES[rank * NODES + source] >> (3 * dest)) & 7
+                for hop, link in enumerate(links_of(source, dest, code)):
+                    table[rank, dest, hop, source] = link + 1
+    return table.reshape(2 * NODES * 8, NODES)
+
+
+def plan_kernel(table_ref, route_ref, length_ref, out_ref, sends):
+    f32 = jnp.float32
+    lane = lax.broadcasted_iota(jnp.int32, (1, 128), 1)
+    route = route_ref[...]
+    source = lane // REQS
+    order = lane % REQS
+    rank = jnp.zeros_like(route)
+    for back in range(1, REQS):
+        earlier = pltpu.roll(route, back, axis=1)
+        rank = rank + jnp.where((earlier == route) & (order >= back), 1, 0)
+    node = lax.broadcasted_iota(jnp.int32, (NODES, 128), 0)
+    count = jnp.sum(jnp.where(node == route, 1.0, 0.0), axis=1, keepdims=True)
+    most = jnp.max(count, axis=0, keepdims=True)
+    nodes = lax.broadcasted_iota(jnp.int32, (NODES, 1), 0).astype(f32)
+    hot = jnp.min(jnp.where(count == most, nodes, 99.0), axis=0, keepdims=True).astype(jnp.int32)
+    hot_z, hot_y = hot // 2, hot % 2
+
+    def relative(x):
+        y = x % 2
+        return ((x // 2 - hot_z + RING) % RING) * 2 + (y + hot_y - 2 * y * hot_y)
+
+    source_rel, dest_rel = relative(source), relative(route)
+    from_one = jnp.where(node == source_rel, 1.0, 0.0).astype(jnp.bfloat16)
+    every = jnp.dot(table_ref[...], from_one, preferred_element_type=f32)
+    row = lax.broadcasted_iota(jnp.int32, (2 * NODES * 8, 128), 0) // 8
+    every = jnp.where(row == rank * NODES + dest_rel, every, 0.0)
+    path = every[0:8]
+    for i in range(1, 2 * NODES):
+        path = path + every[8 * i : 8 * i + 8]
+    me = relative(jnp.zeros((1, 1), jnp.int32) + lax.axis_index("rep"))
+    me_z, me_y = me // 2, me % 2
+    up, down = (me_z + 1) % RING, (me_z + RING - 1) % RING
+    to_me = (down * 2 + me_y, up * 2 + me_y, me_z * 2 + 1 - me_y)
+    out_link = [(me * PORTS + k + 1).astype(f32) for k in range(PORTS)]
+    in_link = [(to_me[k] * PORTS + k + 1).astype(f32) for k in range(PORTS)]
+    link = lax.broadcasted_iota(jnp.int32, (NODES * PORTS, 128), 0).astype(f32) + 1.0
+    tie = (127 - lane).astype(f32)
+    hop_row = lax.broadcasted_iota(jnp.int32, (8, 128), 0)
+    held = jnp.where(source_rel == me, order, 0).astype(f32)
+    sends[...] = jnp.zeros_like(sends)
+    for t in range(ROUNDS):
+        now = path[0:1]
+        left = jnp.sum(jnp.where(path > 0.0, 1.0, 0.0), axis=0, keepdims=True)
+        key = left * 128.0 + tie
+        asks = link == now
+        first = jnp.max(jnp.where(asks, key, -1.0), axis=1, keepdims=True)
+        wins = jnp.where(asks & (first == key), 1.0, 0.0)
+        moves = jnp.max(wins, axis=0, keepdims=True) > 0.0
+        for k in range(PORTS):
+            leaves = moves & (now == out_link[k])
+            sends[PORTS * t + k : PORTS * t + k + 1] = jnp.where(leaves, held, 0.0)
+        for k in range(PORTS):
+            held = jnp.where(moves & (now == in_link[k]), float(REQS + PORTS * t + k), held)
+        later = jnp.where(hop_row < 7, pltpu.roll(path, 7, axis=0), 0.0)
+        path = jnp.where(moves, later, path)
+    left = jnp.sum(jnp.where(path > 0.0, 1.0, 0.0), axis=0, keepdims=True)
+    stuck = jnp.sum(left, axis=1, keepdims=True)
+    square = lax.broadcasted_iota(jnp.int32, (128, 128), 0) == lax.broadcasted_iota(
+        jnp.int32, (128, 128), 1
+    )
+
+    def lay(rows):
+        sums = jnp.sum(rows, axis=1, keepdims=True)
+        n = rows.shape[0]
+        return jnp.sum(jnp.where(square[:n], sums, 0.0), axis=0, keepdims=True)
+
+    slot = lax.broadcasted_iota(jnp.int32, (2 * NODES, 128), 0)
+    mine = (slot == source * 2 + rank) & (dest_rel == me)
+    out = [
+        lay(sends[...]),
+        lay(jnp.where(mine, held, 0.0)),
+        lay(jnp.where(mine, length_ref[...].astype(f32), 0.0)),
+        jnp.where(lane >= 0, jnp.where(stuck > 0.0, 0.0, 1.0), 0.0),
+        jnp.zeros((4, 128), f32),
+    ]
+    out_ref[...] = jnp.concatenate(out, axis=0).astype(jnp.int32)
+
+
+def plan(route, lengths):
+    return pl.pallas_call(
+        plan_kernel,
+        out_shape=jax.ShapeDtypeStruct((8, 128), jnp.int32),
+        in_specs=[pl.BlockSpec(memory_space=pltpu.VMEM)] * 3,
+        out_specs=pl.BlockSpec(memory_space=pltpu.VMEM),
+        scratch_shapes=[pltpu.VMEM((128, 128), jnp.float32)],
+    )(
+        jnp.asarray(path_table(), jnp.bfloat16),
+        route.reshape(1, 128),
+        lengths.reshape(1, 128),
+    )
+
+
+def exchange_kernel(plan_ref, table_ref, pages, scales, *refs):
+    streams = PARTS + 1
+    outs = refs[:streams]
+    groups = refs[streams : 2 * streams]
+    stores = refs[2 * streams : 3 * streams]
+    lands = refs[3 * streams : 4 * streams]
+    packs = refs[4 * streams : 5 * streams]
+    group_send, group_recv, send_sem, recv_sem, out_sem = refs[5 * streams :]
+    rep = lax.axis_index("rep")
+    section = lax.axis_index("section")
+    head = lax.axis_index("head")
+    tokens = groups[0].shape[2]
+    held = pages.shape[2]
+    feats = groups[0].shape[4]
+
+    peers = []
+    for o in range(16):
+        peers.append((lax.rem(section + o // 4, 4), lax.rem(head + o % 4, 4)))
+    neighbours = (
+        lax.rem(rep + 2, NODES),
+        lax.rem(rep + NODES - 2, NODES),
+        rep + 1 - 2 * lax.rem(rep, 2),
+    )
+    barrier = pltpu.get_barrier_semaphore()
+    for s, h in peers[1:]:
+        pl.semaphore_signal(barrier, inc=1, device_id=(rep, s, h), device_id_type=MESH)
+    for n in neighbours:
+        pl.semaphore_signal(barrier, inc=1, device_id=(n, section, head), device_id_type=MESH)
+    pl.semaphore_wait(barrier, 15 + PORTS)
+
+    def block(i, group):
+        if i == PARTS:
+            return scales.at[group]
+        columns = pl.ds(pl.multiple_of(group * feats, 128), feats)
+        return pages.at[0, 0, :, pl.ds(tokens * i, tokens), :, columns]
+
+    def place(i, s, h):
+        return groups[i].at[s, pl.ds(held * h, held)]
+
+    def regroup(i, o):
+        s, h = peers[o]
+        return pltpu.make_async_remote_copy(
+            src_ref=block(i, s * 4 + h),
+            dst_ref=place(i, section, head),
+            send_sem=group_send.at[i, o],
+            recv_sem=group_recv.at[i, o],
+            device_id=(rep, s, h),
+            device_id_type=MESH,
+        )
+
+    def regroup_own(i):
+        return pltpu.make_async_copy(
+            block(i, section * 4 + head), place(i, section, head), group_recv.at[i, 0]
+        )
+
+    order = [PARTS] + list(range(PARTS))
+    for i in order:
+        for o in range(1, 16):
+            regroup(i, o).start()
+        regroup_own(i).start()
+
+    def send(i, slot, k):
+        return pltpu.make_async_remote_copy(
+            src_ref=packs[i].at[slot, k],
+            dst_ref=lands[i].at[slot, k],
+            send_sem=send_sem.at[i, slot, k],
+            recv_sem=recv_sem.at[i, slot, k],
+            device_id=(neighbours[k], section, head),
+            device_id_type=MESH,
+        )
+
+    def write_own(i):
+        return pltpu.make_async_copy(
+            stores[i].at[pl.ds(0, REQS)], outs[i].at[pl.ds(0, REQS)], out_sem.at[i]
+        )
+
+    def write(i, t):
+        rows = pl.ds(REQS + PORTS * t, PORTS)
+        return pltpu.make_async_copy(stores[i].at[rows], outs[i].at[rows], out_sem.at[i])
+
+    def compose(i, t, slot):
+        for k in range(PORTS):
+            packs[i][slot, k] = stores[i][plan_ref[0, PORTS * t + k]]
+        for k in range(PORTS):
+            send(i, slot, k).start()
+
+    def arrive(i, t, slot):
+        for k in range(PORTS):
+            send(i, slot, k).wait_recv()
+        for k in range(PORTS):
+            stores[i][REQS + PORTS * t + k] = lands[i][slot, k]
+
+    for i in order:
+        regroup_own(i).wait()
+        for o in range(1, 16):
+            regroup(i, o).wait_recv()
+        for q in range(REQS):
+            for j in range(2):
+                stores[i][q, :, j] = groups[i][:, table_ref[0, 2 * q + j]]
+        write_own(i).start()
+        compose(i, 0, 0)
+
+    for i in order:
+        arrive(i, 0, 0)
+        write_own(i).wait()
+        write(i, 0).start()
+        compose(i, 1, 1)
+
+    def one(t, carry):
+        slot = lax.rem(t, 2)
+        for i in order:
+            arrive(i, t - 1, 1 - slot)
+            write(i, t - 2).wait()
+            write(i, t - 1).start()
+            for k in range(PORTS):
+                send(i, slot, k).wait_send()
+            compose(i, t, slot)
+        return carry
+
+    lax.fori_loop(2, ROUNDS, one, 0)
+    for i in order:
+        arrive(i, ROUNDS - 1, (ROUNDS - 1) % 2)
+        write(i, ROUNDS - 2).wait()
+        write(i, ROUNDS - 1).start()
+    for i in order:
+        write(i, ROUNDS - 1).wait()
+        for slot in range(2):
+            for k in range(PORTS):
+                send(i, slot, k).wait_send()
+        for o in range(1, 16):
+            regroup(i, o).wait_send()
+
+
+def exchange(steps, page_table, pages, scales):
+    layers = 4
+    held = pages.shape[2]
+    tokens = pages.shape[3] // PARTS
+    feats = pages.shape[5] // 16
+    units = [(tokens, 2, feats)] * PARTS + [(2, 128)]
+    bf16 = jnp.bfloat16
+    anywhere = pl.BlockSpec(memory_space=pl.ANY)
+    smem = pl.BlockSpec(memory_space=pltpu.SMEM)
+    scratch = [pltpu.VMEM((layers, 4 * held) + u, bf16) for u in units]
+    scratch += [pltpu.VMEM((STORE, layers, 2) + u, bf16) for u in units]
+    scratch += [pltpu.VMEM((2, PORTS, layers, 2) + u, bf16) for u in units] * 2
+    dma = pltpu.SemaphoreType.DMA
+    streams = PARTS + 1
+    scratch += [dma((streams, 16)), dma((streams, 16))]
+    scratch += [dma((streams, 2, PORTS)), dma((streams, 2, PORTS)), dma((streams,))]
+    return pl.pallas_call(
+        exchange_kernel,
+        out_shape=[jax.ShapeDtypeStruct((STORE, layers, 2) + u, bf16) for u in units],
+        in_specs=[smem, smem, anywhere, anywhere],
+        out_specs=[anywhere] * streams,
+        scratch_shapes=scratch,
+        compiler_params=pltpu.CompilerParams(
+            collective_id=1, has_side_effects=True, vmem_limit_bytes=40 << 20
+        ),
+        cost_estimate=pl.CostEstimate(flops=0, bytes_accessed=20 << 20, transcendentals=0),
+    )(steps, page_table, pages, scales)
+
+
+def attend_kernel(plan_ref, *refs):
+    units, scale_ref = refs[:PARTS], refs[PARTS]
+    query_ref, new_ref, cache_ref, scales_ref, att_ref = refs[PARTS + 1 :]
+    i = pl.program_id(0)
+    span = plan_ref[2, i]
+    layers = query_ref.shape[1]
+    steps, feats = query_ref.shape[4], query_ref.shape[5]
+    heads = feats // 128
+    tokens = units[0].shape[3]
+    span_max = cache_ref.shape[4]
+    rows = heads * steps
+    f32 = jnp.float32
+
+    @pl.when(span == 0)
+    def _():
+        cache_ref[...] = jnp.zeros_like(cache_ref)
+        scales_ref[...] = jnp.zeros_like(scales_ref)
+        att_ref[...] = jnp.zeros_like(att_ref)
+
+    @pl.when(span > 0)
+    def _():
+        row = lax.broadcasted_iota(jnp.int32, (rows, 128), 0)
+        column = lax.broadcasted_iota(jnp.int32, (rows, 128), 1)
+        place = column // 2
+        even = column % 2 == 0
+        prompt = (column < 2 * span_max) & (place < span)
+        fresh = (column >= 2 * span_max) & (place - span_max <= row % steps)
+        valid = even & (prompt | fresh)
+        own_head = jnp.where(column == row // steps, 1.0, 0.0).astype(jnp.bfloat16)
+        block = lax.broadcasted_iota(jnp.int32, (rows, feats), 1) // 128
+        block = block == lax.broadcasted_iota(jnp.int32, (rows, feats), 0) // steps
+        root = math.sqrt(128)
+        spare = 128 - 2 * span_max - 2 * steps
+        for l in range(layers):
+            for j in range(2):
+                for s in range(PARTS):
+                    at = 16 * j + tokens * s
+                    cache_ref[0, l, 0, 0, at : at + tokens] = units[s][0, l, j]
+            scales_ref[0, l, 0, 0] = scale_ref[0, l][:, :, :heads]
+            known = cache_ref[0, l, 0, 0].reshape(2 * span_max, feats)
+            new = new_ref[0, l, 0, 0].reshape(2 * steps, feats)
+            both = jnp.concatenate([known, new, jnp.zeros((spare, feats), known.dtype)], axis=0)
+            query = query_ref[0, l, 0, 0].astype(f32)
+            query = jnp.concatenate([query] * heads, axis=0)
+            query = jnp.where(block, query, 0.0).astype(jnp.bfloat16)
+            over = (((1,), (1,)), ((), ()))
+            score = lax.dot_general(query, both, over, preferred_element_type=f32)
+            scale = [
+                jnp.broadcast_to(scale_ref[0, l, j][None], (16, 2, 128)).reshape(32, 128)
+                for j in range(2)
+            ]
+            scale.append(jnp.ones((128 - 2 * span_max, 128), jnp.bfloat16))
+            scale = jnp.concatenate(scale, axis=0)
+            scale = lax.dot_general(own_head, scale, over, preferred_element_type=f32)
+            score = jnp.where(valid, score * scale / root, -jnp.inf)
+            top = jnp.max(score, axis=1, keepdims=True)
+            power = jnp.exp(score - top)
+            total = jnp.sum(power, axis=1, keepdims=True)
+            weight = (pltpu.roll(power, 1, axis=1) * scale / total).astype(jnp.bfloat16)
+            result = jnp.dot(weight, both, preferred_element_type=f32)
+            for h in range(heads):
+                part = result[steps * h : steps * h + steps, 128 * h : 128 * h + 128]
+                att_ref[0, l, 0, 0, :, 128 * h : 128 * h + 128] = part.astype(att_ref.dtype)
+
+
+def attend(steps, stores, queries, new_kv):
+    layers, nodes, cap, step_count, feats = queries.shape[1:]
+    heads = feats // 128
+    span_max = 32
+    bf16 = jnp.bfloat16
+
+    def unit(shape):
+        rest = (0,) * (len(shape) - 1)
+        return pl.BlockSpec((1,) + shape[1:], lambda i, p: (p[1, i],) + rest)
+
+    def slot(shape):
+        rest = (0,) * (len(shape) - 4)
+        return pl.BlockSpec(
+            (1, layers, 1, 1) + shape[4:], lambda i, p: (0, 0, i // cap, i % cap) + rest
+        )
+
+    outs = [
+        (1, layers, nodes, cap, span_max, 2, feats),
+        (1, layers, nodes, cap, 2, 2, heads),
+        queries.shape,
+    ]
+    return pl.pallas_call(
+        attend_kernel,
+        grid_spec=pltpu.PrefetchScalarGridSpec(
+            num_scalar_prefetch=1,
+            grid=(nodes * cap,),
+            in_specs=[unit(s.shape) for s in stores] + [slot(queries.shape), slot(new_kv.shape)],
+            out_specs=[slot(s) for s in outs],
+        ),
+        out_shape=[jax.ShapeDtypeStruct(s, bf16) for s in outs],
+        compiler_params=pltpu.CompilerParams(vmem_limit_bytes=40 << 20),
+    )(steps, *stores, queries, new_kv)
 
 
 def slot_ranks(route):
@@ -13,7 +421,7 @@
     return jnp.sum((same_dest & earlier[None]).astype(jnp.int32), axis=2)
 
 
-def body(prompt_pages, page_scales, page_table, lengths, route, queries, new_kv):
+def padded(prompt_pages, page_scales, page_table, lengths, route, queries, new_kv):
     rep_count = lax.axis_size("rep")
     section_count = lax.axis_size("section")
     head_count = lax.axis_size("head")
@@ -160,6 +568,30 @@
     )
 
 
+def body(prompt_pages, page_scales, page_table, lengths, route, queries, new_kv):
+    steps = plan(route, lengths)
+
+    def direct(prompt_pages, page_scales, page_table, lengths, route, queries, new_kv):
+        held = page_scales.shape[2]
+        scales = page_scales.reshape(held, 2, 16, -1).transpose(2, 0, 1, 3)
+        scales = jnp.pad(scales, ((0, 0), (0, 0), (0, 0), (0, 128 - scales.shape[3])))
+        stores = exchange(steps, page_table, prompt_pages, scales)
+        return tuple(attend(steps, stores, queries, new_kv))
+
+    return lax.cond(
+        steps[3, 0] > 0,
+        direct,
+        padded,
+        prompt_pages,
+        page_scales,
+        page_table,
+        lengths,
+        route,
+        queries,
+        new_kv,
+    )
+
+
 def solution(mesh):
     return jax.shard_map(
         body,

time: 290 us -> 172 us (0.59)
  waiting for transfers between devices: 169 us -> 0 us
  Pallas kernels: 0 us -> 164 us
  local copies, waits for them, and re-layouts: 63.2 us -> 5.35 us
  starting transfers between devices: 37.5 us -> 0 us
  matrix products: 9.44 us -> 0 us
  other arithmetic: 8.86 us -> 0 us
    all_to_all x6 -> x0, waiting for transfers between devices: 169 us -> none  [the longest x1 134 us: body(): lax.all_to_all(slot_pages, 'rep', split_axis=1, concat_axis=1, tiled=True)]
    pallas_call x0 -> x3, Pallas kernels: none -> 164 us  [the longest x1 105 us: exchange(): pl.pallas_call(exchange_kernel, out_shape=[jax.ShapeDtypeStruct((STORE, l...]
    all_to_all x6 -> x0, starting transfers between devices: 37.5 us -> none  [the longest x1 10.2 us: body(): lax.all_to_all(slot_scales, 'rep', split_axis=1, concat_axis=1, tiled=True)]
    another operation x6 -> x0, local copies, waits for them, and re-layouts: 26.1 us -> none  [the longest x1 9 us: body(): page_cache[:, :, :, :, 0, :]]
    all_to_all x6 -> x0, local copies, waits for them, and re-layouts: 19.5 us -> none  [the longest x2 14.2 us: body(): lax.all_to_all(slot_pages, 'rep', split_axis=1, concat_axis=1, tiled=True)]
    dot_general x4 -> x0, matrix products: 9.44 us -> none  [the longest x1 4.1 us: body(): jnp.einsum('lrcthd,lrckhd->lrchtk', query_rows, prompt_keys, preferred_el...]
    select_n x4 -> x0, other arithmetic: 6.41 us -> none  [the longest x2 6.16 us: body(): slot_pages = jnp.where(live_mask, all_pages[:, physical], zero_page)]
    gather x5 -> x0, local copies, waits for them, and re-layouts: 5.83 us -> none  [the longest x1 4.14 us: body(): slot_pages = jnp.where(live_mask, all_pages[:, physical], zero_page)]
  transfers between devices with their start and end apart: 6 -> 0, of which waited for: 4 -> 0; matrix products, arithmetic and copies ran while one was open for 11% -> 0% of each run, Pallas kernels for 0% -> 0%
where the time goes in v1:
time: 172 us; the launch traced here: 171 us
  Pallas kernels  164 us (95%)
  local copies, waits for them, and re-layouts  5.35 us (3%)
    pallas_call x1, Pallas kernels, exchange(): pl.pallas_call(exchange_kernel, out_shape=[jax.ShapeDtypeStruct((STORE, l...  105 us
    pallas_call x1, Pallas kernels, attend(): pl.pallas_call(attend_kernel, grid_spec=pltpu.PrefetchScalarGridSpec(num_...  56.1 us

profile of v1, /device:TPU:2, one launch (start us, length us, event | category | flops | bytes accessed | tf_op | source)
XLA Modules:
  0.0 170.5 jit_solution(12565052445140047409)
XLA Ops:
  0.6 0.8 copy.154
  1.4 0.6 reshape.190.route_ref
  2.0 0.8 copy.155
  2.7 0.6 reshape.191.length_ref
  3.4 2.8 %shard_map.109 = s32[8,128]{1,0:T(8,128)S(1)} custom-call(bf16[256,16]{1,0:T(8,128)(2,1)} %constant.39.clone.table_ref, s32[1,128]{1,0:T(1,128)} %reshape.190.route_ref, s32[1,128]{1,0:T(1,128)} %reshape.191.length_ref), custom_call_target="tpu_custom_call" | custom-call | tf_op jit(solution)/shard_map/pallas_call | solution.py:143
  6.2 0.5 slice.21
  7.4 162.3 %conditional.1 = (bf16[1,4,16,2,32,2,384]{6,5,4,3,2,1,0:T(2,128)(2,1)}, bf16[1,4,16,2,8,384]{5,4,3,2,1,0:T(8,128)(2,1)S(1)}, bf16[1,4,16,2,2,2,3]{2,5,6,4,3,1,0:T(2,128)(2,1)S(1)}) conditional(s32[]{:T(128)} %bitcast.36, (s32[16,8]{0,1:T(8,128)}, bf16[1,1,4,16,2,6144]{5,4,3,2,1,0:T(2,128)(2,1)}, s32[1,16]{1,0:T(1,128)}, ...), branch_computations={%region_0.10_spmd, %region_10.11_spmd} | conditional | flops 68673144 | bytes 169585952 | solution.py:581
  7.6 0.0 copy-start.2
  7.6 0.9 reshape.187
  8.6 104.7 %branch_1_fun.2 = (bf16[56,4,2,4,2,384]{5,4,3,2,1,0:T(2,128)(2,1)S(1)}, bf16[56,4,2,4,2,384]{5,4,3,2,1,0:T(2,128)(2,1)S(1)}, bf16[56,4,2,4,2,384]{5,4,3,2,1,0:T(...) custom-call(s32[8,128]{1,0:T(8,128)S(1)} %get-tuple-element.33.plan_ref, ...), custom_call_target="tpu_custom_call" | custom-call | bytes 20971520 | tf_op jit(solution)/shard_map/cond/branch_1_fun/pallas_call | solution.py:305
  113.3 0.0 copy-done.2
  113.3 56.1 %branch_1_fun.3 = (bf16[1,4,16,2,32,2,384]{6,5,4,3,2,1,0:T(2,128)(2,1)}, bf16[1,4,16,2,2,2,3]{6,5,4,3,2,1,0:T(2,128)(2,1)S(1)}, bf16[1,4,16,2,8,384]{5,4,3,2,1,0:T(8,128)(2,1)S(1)}) custom-call(s32[8,128]{1,0:T(8,128)S(1)} %get-tuple-element.33.plan_ref, bf16[56,4,2,4,2,384]{5,4,3,2,1,0:T(2,128)(2,1)S(1)} %get-tuple-element.37.refs_0_, ...), custom_call_target="tpu_custom_call" | custom-call | tf_op jit(solution)/shard_map/cond/branch_1_fun/pallas_call | solution.py:404
  169.4 0.3 copy.165
  169.6 0.0 copy-start.9
  169.6 0.0 copy-start.11
  169.6 0.6 copy-done.9
  170.2 0.3 copy-done.11
  (2 shorter events, 0.1 us)
Async XLA Ops:
  7.6 105.7 %copy-start.2 = (bf16[1,4,16,2,8,2,384]{6,5,4,3,2,1,0:T(2,128)(2,1)S(1)}, bf16[1,4,16,2,8,2,384]{6,5,4,3,2,1,0:T(2,128)(2,1)}, u32[]{:S(2)}) copy-start(bf16[1,4,16,2,8,2,384]{6,5,4,3,2,1,0:T(2,128)(2,1)} %get-tuple-element.43.refs_6_) | copy-start | bytes 4718596 | tf_op jit(solution)/shard_map/cond
  169.6 0.6 copy-start.9
  169.6 0.9 copy-start.11

commit v2 on v1

--- a/solution.py
+++ b/solution.py
@@ -15,6 +15,7 @@
 ROUNDS = 16
 PARTS = 4
 REQS = 8
+PAGE = 16
 STORE = REQS + PORTS * ROUNDS
 
 ROUTES = (
@@ -61,17 +62,27 @@
     return table.reshape(2 * NODES * 8, NODES)
 
 
-def plan_kernel(table_ref, route_ref, length_ref, out_ref, sends):
+def plan_kernel(table_ref, route_ref, length_ref, out_ref, sends, slots, spans):
     f32 = jnp.float32
     lane = lax.broadcasted_iota(jnp.int32, (1, 128), 1)
-    route = route_ref[...]
     source = lane // REQS
     order = lane % REQS
+    pick = lax.broadcasted_iota(jnp.int32, (REQS, 128), 1) % REQS
+    pick = pick == lax.broadcasted_iota(jnp.int32, (REQS, 128), 0)
+    pick = jnp.where(pick, 1.0, 0.0).astype(jnp.bfloat16)
+
+    def flat(ref):
+        x = jnp.dot(ref[...].astype(jnp.bfloat16), pick, preferred_element_type=f32)
+        x = jnp.where(node == source, x, 0.0)
+        return jnp.sum(x, axis=0, keepdims=True)
+
+    node = lax.broadcasted_iota(jnp.int32, (NODES, 128), 0)
+    route = flat(route_ref).astype(jnp.int32)
+    length = flat(length_ref)
     rank = jnp.zeros_like(route)
     for back in range(1, REQS):
         earlier = pltpu.roll(route, back, axis=1)
         rank = rank + jnp.where((earlier == route) & (order >= back), 1, 0)
-    node = lax.broadcasted_iota(jnp.int32, (NODES, 128), 0)
     count = jnp.sum(jnp.where(node == route, 1.0, 0.0), axis=1, keepdims=True)
     most = jnp.max(count, axis=0, keepdims=True)
     nodes = lax.broadcasted_iota(jnp.int32, (NODES, 1), 0).astype(f32)
@@ -100,7 +111,11 @@
     tie = (127 - lane).astype(f32)
     hop_row = lax.broadcasted_iota(jnp.int32, (8, 128), 0)
     held = jnp.where(source_rel == me, order, 0).astype(f32)
-    sends[...] = jnp.zeros_like(sends)
+    home = dest_rel == me
+    own_slot = jnp.where(home, source * 2 + rank, 0).astype(f32)
+    own_span = jnp.where(home, length, 0.0)
+    for ref in (sends, slots, spans):
+        ref[...] = jnp.zeros_like(ref)
     for t in range(ROUNDS):
         now = path[0:1]
         left = jnp.sum(jnp.where(path > 0.0, 1.0, 0.0), axis=0, keepdims=True)
@@ -113,7 +128,10 @@
             leaves = moves & (now == out_link[k])
             sends[PORTS * t + k : PORTS * t + k + 1] = jnp.where(leaves, held, 0.0)
         for k in range(PORTS):
-            held = jnp.where(moves & (now == in_link[k]), float(REQS + PORTS * t + k), held)
+            comes = moves & (now == in_link[k])
+            held = jnp.where(comes, float(REQS + PORTS * t + k), held)
+            slots[PORTS * t + k : PORTS * t + k + 1] = jnp.where(comes, own_slot, 0.0)
+            spans[PORTS * t + k : PORTS * t + k + 1] = jnp.where(comes, own_span, 0.0)
         later = jnp.where(hop_row < 7, pltpu.roll(path, 7, axis=0), 0.0)
         path = jnp.where(moves, later, path)
     left = jnp.sum(jnp.where(path > 0.0, 1.0, 0.0), axis=0, keepdims=True)
@@ -128,13 +146,15 @@
         return jnp.sum(jnp.where(square[:n], sums, 0.0), axis=0, keepdims=True)
 
     slot = lax.broadcasted_iota(jnp.int32, (2 * NODES, 128), 0)
-    mine = (slot == source * 2 + rank) & (dest_rel == me)
+    mine = (slot == source * 2 + rank) & home
     out = [
         lay(sends[...]),
         lay(jnp.where(mine, held, 0.0)),
-        lay(jnp.where(mine, length_ref[...].astype(f32), 0.0)),
+        lay(jnp.where(mine, length, 0.0)),
         jnp.where(lane >= 0, jnp.where(stuck > 0.0, 0.0, 1.0), 0.0),
-        jnp.zeros((4, 128), f32),
+        lay(slots[...]),
+        lay(spans[...]),
+        jnp.zeros((2, 128), f32),
     ]
     out_ref[...] = jnp.concatenate(out, axis=0).astype(jnp.int32)
 
@@ -145,28 +165,86 @@
         out_shape=jax.ShapeDtypeStruct((8, 128), jnp.int32),
         in_specs=[pl.BlockSpec(memory_space=pltpu.VMEM)] * 3,
         out_specs=pl.BlockSpec(memory_space=pltpu.VMEM),
-        scratch_shapes=[pltpu.VMEM((128, 128), jnp.float32)],
-    )(
-        jnp.asarray(path_table(), jnp.bfloat16),
-        route.reshape(1, 128),
-        lengths.reshape(1, 128),
-    )
-
-
-def exchange_kernel(plan_ref, table_ref, pages, scales, *refs):
+        scratch_shapes=[pltpu.VMEM((128, 128), jnp.float32)] * 3,
+    )(jnp.asarray(path_table(), jnp.bfloat16), route, lengths)
+
+
+def attend(known, new, queries, scale, span):
+    f32 = jnp.float32
+    bf16 = jnp.bfloat16
+    layers = len(known)
+    steps, feats = queries[0].shape
+    heads = feats // 128
+    rows = known[0].shape[0]
+    total_rows = rows + new[0].shape[0]
+    per_layer = heads * steps
+    over = (((1,), (1,)), ((), ()))
+    row = lax.broadcasted_iota(jnp.int32, (total_rows, 128), 0)
+    lane = lax.broadcasted_iota(jnp.int32, (total_rows, 128), 1)
+    even = row % 2 == 0
+    part = rows // PARTS
+    page = row % part // (part // 2)
+    token = PAGE * page + row // part * (PAGE // PARTS) + row % (part // 2) // 2
+    fresh = (row >= rows) & ((row - rows) // 2 <= lane % steps)
+    valid = even & (((row < rows) & (token < span)) | fresh)
+    own_head = lax.broadcasted_iota(jnp.int32, (128, 128), 0)
+    own_head = own_head == lax.broadcasted_iota(jnp.int32, (128, 128), 1) // steps
+    own_head = jnp.where(own_head, 1.0, 0.0).astype(bf16)
+    block = lax.broadcasted_iota(jnp.int32, (per_layer, feats), 1) // 128
+    block = block == lax.broadcasted_iota(jnp.int32, (per_layer, feats), 0) // steps
+
+    both = [jnp.concatenate([known[l], new[l]], axis=0) for l in range(layers)]
+    query = []
+    for one in queries:
+        one = jnp.concatenate([one.astype(f32)] * heads, axis=0)
+        query.append(jnp.where(block, one, 0.0))
+    query.append(jnp.zeros((128 - layers * per_layer, feats), f32))
+    query = jnp.concatenate(query, axis=0).astype(bf16)
+    score = lax.dot_general(both[0], query, over, preferred_element_type=f32)
+    for l in range(1, layers):
+        other = lax.dot_general(both[l], query, over, preferred_element_type=f32)
+        score = jnp.where(lane // per_layer == l, other, score)
+    scale = scale.astype(f32)
+    scale = ((scale[0] + scale[1]) + (scale[2] + scale[3])).reshape(4, 128)
+    scale = jnp.concatenate([scale, jnp.zeros((12, 128), f32)], axis=0).astype(bf16)
+    scale = jnp.dot(scale, own_head, preferred_element_type=f32)
+    factor = jnp.where(
+        page == 0,
+        jnp.where(even, scale[0:1], scale[1:2]),
+        jnp.where(even, scale[2:3], scale[3:4]),
+    )
+    factor = jnp.where(row < rows, factor, 1.0)
+    score = jnp.where(valid, score * factor / math.sqrt(128), -jnp.inf)
+    power = jnp.exp(score - jnp.max(score, axis=0, keepdims=True))
+    total = jnp.sum(power, axis=0, keepdims=True)
+    weight = (pltpu.roll(power, 1, axis=0) * factor / total).T
+    results = []
+    for l in range(layers):
+        own = weight[per_layer * l : per_layer * (l + 1)].astype(bf16)
+        result = jnp.dot(own, both[l], preferred_element_type=f32)
+        parts = [
+            result[steps * h : steps * h + steps, 128 * h : 128 * h + 128] for h in range(heads)
+        ]
+        results.append(jnp.concatenate(parts, axis=1).astype(bf16))
+    return results
+
+
+def exchange_kernel(plan_ref, table_ref, pages, scales, query_hbm, new_hbm, *refs):
     streams = PARTS + 1
-    outs = refs[:streams]
-    groups = refs[streams : 2 * streams]
-    stores = refs[2 * streams : 3 * streams]
-    lands = refs[3 * streams : 4 * streams]
-    packs = refs[4 * streams : 5 * streams]
-    group_send, group_recv, send_sem, recv_sem, out_sem = refs[5 * streams :]
+    stores = refs[:streams]
+    att = refs[streams]
+    refs = refs[streams + 1 :]
+    groups = refs[:streams]
+    lands = refs[streams : 2 * streams]
+    packs = refs[2 * streams : 3 * streams]
+    queries, news, group_send, group_recv, send_sem, recv_sem, new_sem = refs[3 * streams :]
     rep = lax.axis_index("rep")
     section = lax.axis_index("section")
     head = lax.axis_index("head")
     tokens = groups[0].shape[2]
     held = pages.shape[2]
     feats = groups[0].shape[4]
+    layers, _, steps, _ = queries.shape
 
     peers = []
     for o in range(16):
@@ -213,6 +291,10 @@
         for o in range(1, 16):
             regroup(i, o).start()
         regroup_own(i).start()
+    load_query = pltpu.make_async_copy(query_hbm, queries, new_sem.at[0])
+    load_new = pltpu.make_async_copy(new_hbm, news, new_sem.at[1])
+    load_query.start()
+    load_new.start()
 
     def send(i, slot, k):
         return pltpu.make_async_remote_copy(
@@ -224,15 +306,6 @@
             device_id_type=MESH,
         )
 
-    def write_own(i):
-        return pltpu.make_async_copy(
-            stores[i].at[pl.ds(0, REQS)], outs[i].at[pl.ds(0, REQS)], out_sem.at[i]
-        )
-
-    def write(i, t):
-        rows = pl.ds(REQS + PORTS * t, PORTS)
-        return pltpu.make_async_copy(stores[i].at[rows], outs[i].at[rows], out_sem.at[i])
-
     def compose(i, t, slot):
         for k in range(PORTS):
             packs[i][slot, k] = stores[i][plan_ref[0, PORTS * t + k]]
@@ -244,6 +317,29 @@
             send(i, slot, k).wait_recv()
         for k in range(PORTS):
             stores[i][REQS + PORTS * t + k] = lands[i][slot, k]
+
+    def attend_unit(at, unit, slot, span):
+        known = [
+            jnp.concatenate(
+                [stores[i][unit, l].reshape(4 * tokens, feats) for i in range(PARTS)], axis=0
+            )
+            for l in range(layers)
+        ]
+        new = [news[l, slot].reshape(2 * steps, feats) for l in range(layers)]
+        query = [queries[l, slot] for l in range(layers)]
+        results = attend(known, new, query, stores[PARTS][unit], span)
+        for l in range(layers):
+            att[at, l] = results[l]
+
+    def attend_own():
+        for c in range(2):
+            slot = 2 * rep + c
+            attend_unit(c, plan_ref[1, slot], slot, plan_ref[2, slot])
+
+    def attend_arrived(t):
+        for k in range(PORTS):
+            at = PORTS * t + k
+            attend_unit(REQS + at, REQS + at, plan_ref[4, at], plan_ref[5, at])
 
     for i in order:
         regroup_own(i).wait()
@@ -252,33 +348,31 @@
         for q in range(REQS):
             for j in range(2):
                 stores[i][q, :, j] = groups[i][:, table_ref[0, 2 * q + j]]
-        write_own(i).start()
         compose(i, 0, 0)
+    load_query.wait()
+    load_new.wait()
+    attend_own()
 
     for i in order:
         arrive(i, 0, 0)
-        write_own(i).wait()
-        write(i, 0).start()
         compose(i, 1, 1)
+    attend_arrived(0)
 
     def one(t, carry):
         slot = lax.rem(t, 2)
         for i in order:
             arrive(i, t - 1, 1 - slot)
-            write(i, t - 2).wait()
-            write(i, t - 1).start()
             for k in range(PORTS):
                 send(i, slot, k).wait_send()
             compose(i, t, slot)
+        attend_arrived(t - 1)
         return carry
 
     lax.fori_loop(2, ROUNDS, one, 0)
     for i in order:
         arrive(i, ROUNDS - 1, (ROUNDS - 1) % 2)
-        write(i, ROUNDS - 2).wait()
-        write(i, ROUNDS - 1).start()
+    attend_arrived(ROUNDS - 1)
     for i in order:
-        write(i, ROUNDS - 1).wait()
         for slot in range(2):
             for k in range(PORTS):
                 send(i, slot, k).wait_send()
@@ -286,132 +380,115 @@
             regroup(i, o).wait_send()
 
 
-def exchange(steps, page_table, pages, scales):
-    layers = 4
+def exchange(steps, page_table, pages, scales, queries, new_kv):
+    layers, nodes, cap, step_count, feats = queries.shape[1:]
     held = pages.shape[2]
     tokens = pages.shape[3] // PARTS
-    feats = pages.shape[5] // 16
     units = [(tokens, 2, feats)] * PARTS + [(2, 128)]
     bf16 = jnp.bfloat16
     anywhere = pl.BlockSpec(memory_space=pl.ANY)
     smem = pl.BlockSpec(memory_space=pltpu.SMEM)
+    vmem = pl.BlockSpec(memory_space=pltpu.VMEM)
     scratch = [pltpu.VMEM((layers, 4 * held) + u, bf16) for u in units]
-    scratch += [pltpu.VMEM((STORE, layers, 2) + u, bf16) for u in units]
     scratch += [pltpu.VMEM((2, PORTS, layers, 2) + u, bf16) for u in units] * 2
+    query_shape = (layers, nodes * cap, step_count, feats)
+    new_shape = (layers, nodes * cap, step_count, 2, feats)
+    scratch += [pltpu.VMEM(query_shape, bf16), pltpu.VMEM(new_shape, bf16)]
     dma = pltpu.SemaphoreType.DMA
     streams = PARTS + 1
     scratch += [dma((streams, 16)), dma((streams, 16))]
-    scratch += [dma((streams, 2, PORTS)), dma((streams, 2, PORTS)), dma((streams,))]
+    scratch += [dma((streams, 2, PORTS)), dma((streams, 2, PORTS)), dma((2,))]
     return pl.pallas_call(
         exchange_kernel,
-        out_shape=[jax.ShapeDtypeStruct((STORE, layers, 2) + u, bf16) for u in units],
-        in_specs=[smem, smem, anywhere, anywhere],
-        out_specs=[anywhere] * streams,
+        out_shape=[jax.ShapeDtypeStruct((STORE, layers, 2) + u, bf16) for u in units]
+        + [jax.ShapeDtypeStruct((STORE, layers, step_count, feats), bf16)],
+        in_specs=[smem, smem] + [anywhere] * 4,
+        out_specs=[vmem] * (streams + 1),
         scratch_shapes=scratch,
         compiler_params=pltpu.CompilerParams(
             collective_id=1, has_side_effects=True, vmem_limit_bytes=40 << 20
         ),
         cost_estimate=pl.CostEstimate(flops=0, bytes_accessed=20 << 20, transcendentals=0),
-    )(steps, page_table, pages, scales)
-
-
-def attend_kernel(plan_ref, *refs):
-    units, scale_ref = refs[:PARTS], refs[PARTS]
-    query_ref, new_ref, cache_ref, scales_ref, att_ref = refs[PARTS + 1 :]
-    i = pl.program_id(0)
-    span = plan_ref[2, i]
-    layers = query_ref.shape[1]
-    steps, feats = query_ref.shape[4], query_ref.shape[5]
-    heads = feats // 128
+    )(
+        steps,
+        page_table,
+        pages,
+        scales,
+        queries.reshape(query_shape),
+        new_kv.reshape(new_shape),
+    )
+
+
+def place_kernel(plan_ref, *refs):
+    units, scales, att = refs[:PARTS], refs[PARTS], refs[PARTS + 1]
+    cache_hbm, scales_ref, att_hbm, zero_unit, zero_att, sems = refs[PARTS + 2 :]
+    layers, slots, _, _, heads = scales_ref.shape
     tokens = units[0].shape[3]
-    span_max = cache_ref.shape[4]
-    rows = heads * steps
-    f32 = jnp.float32
-
-    @pl.when(span == 0)
-    def _():
-        cache_ref[...] = jnp.zeros_like(cache_ref)
-        scales_ref[...] = jnp.zeros_like(scales_ref)
-        att_ref[...] = jnp.zeros_like(att_ref)
-
-    @pl.when(span > 0)
-    def _():
-        row = lax.broadcasted_iota(jnp.int32, (rows, 128), 0)
-        column = lax.broadcasted_iota(jnp.int32, (rows, 128), 1)
-        place = column // 2
-        even = column % 2 == 0
-        prompt = (column < 2 * span_max) & (place < span)
-        fresh = (column >= 2 * span_max) & (place - span_max <= row % steps)
-        valid = even & (prompt | fresh)
-        own_head = jnp.where(column == row // steps, 1.0, 0.0).astype(jnp.bfloat16)
-        block = lax.broadcasted_iota(jnp.int32, (rows, feats), 1) // 128
-        block = block == lax.broadcasted_iota(jnp.int32, (rows, feats), 0) // steps
-        root = math.sqrt(128)
-        spare = 128 - 2 * span_max - 2 * steps
-        for l in range(layers):
-            for j in range(2):
-                for s in range(PARTS):
-                    at = 16 * j + tokens * s
-                    cache_ref[0, l, 0, 0, at : at + tokens] = units[s][0, l, j]
-            scales_ref[0, l, 0, 0] = scale_ref[0, l][:, :, :heads]
-            known = cache_ref[0, l, 0, 0].reshape(2 * span_max, feats)
-            new = new_ref[0, l, 0, 0].reshape(2 * steps, feats)
-            both = jnp.concatenate([known, new, jnp.zeros((spare, feats), known.dtype)], axis=0)
-            query = query_ref[0, l, 0, 0].astype(f32)
-            query = jnp.concatenate([query] * heads, axis=0)
-            query = jnp.where(block, query, 0.0).astype(jnp.bfloat16)
-            over = (((1,), (1,)), ((), ()))
-            score = lax.dot_general(query, both, over, preferred_element_type=f32)
-            scale = [
-                jnp.broadcast_to(scale_ref[0, l, j][None], (16, 2, 128)).reshape(32, 128)
-                for j in range(2)
-            ]
-            scale.append(jnp.ones((128 - 2 * span_max, 128), jnp.bfloat16))
-            scale = jnp.concatenate(scale, axis=0)
-            scale = lax.dot_general(own_head, scale, over, preferred_element_type=f32)
-            score = jnp.where(valid, score * scale / root, -jnp.inf)
-            top = jnp.max(score, axis=1, keepdims=True)
-            power = jnp.exp(score - top)
-            total = jnp.sum(power, axis=1, keepdims=True)
-            weight = (pltpu.roll(power, 1, axis=1) * scale / total).astype(jnp.bfloat16)
-            result = jnp.dot(weight, both, preferred_element_type=f32)
-            for h in range(heads):
-                part = result[steps * h : steps * h + steps, 128 * h : 128 * h + 128]
-                att_ref[0, l, 0, 0, :, 128 * h : 128 * h + 128] = part.astype(att_ref.dtype)
-
-
-def attend(steps, stores, queries, new_kv):
+    cap = 2
+    rep = lax.axis_index("rep")
+    zero_unit[...] = jnp.zeros_like(zero_unit)
+    zero_att[...] = jnp.zeros_like(zero_att)
+
+    def copies(i, live):
+        unit = plan_ref[1, i]
+        at = jnp.where(i // cap == rep, i % cap, unit)
+        out = []
+        for s in range(PARTS):
+            to = cache_hbm.at[0, :, i // cap, i % cap, :, pl.ds(tokens * s, tokens)]
+            source = units[s].at[unit] if live else zero_unit
+            out.append(pltpu.make_async_copy(source, to, sems.at[i, s]))
+        source = att.at[at] if live else zero_att
+        to = att_hbm.at[0, :, i // cap, i % cap]
+        return out + [pltpu.make_async_copy(source, to, sems.at[i, PARTS])]
+
+    @pl.loop(0, slots)
+    def _(i):
+        @pl.when(plan_ref[2, i] > 0)
+        def _():
+            for copy in copies(i, True):
+                copy.start()
+            scale = scales[plan_ref[1, i]]
+            for l in range(layers):
+                scales_ref[l, i] = scale[l][:, :, heads * l : heads * l + heads]
+
+        @pl.when(plan_ref[2, i] == 0)
+        def _():
+            for copy in copies(i, False):
+                copy.start()
+            for l in range(layers):
+                scales_ref[l, i] = jnp.zeros((2, 2, heads), scales_ref.dtype)
+
+    @pl.loop(0, slots)
+    def _(i):
+        for copy in copies(i, False):
+            copy.wait()
+
+
+def place(steps, units, queries):
     layers, nodes, cap, step_count, feats = queries.shape[1:]
     heads = feats // 128
-    span_max = 32
     bf16 = jnp.bfloat16
-
-    def unit(shape):
-        rest = (0,) * (len(shape) - 1)
-        return pl.BlockSpec((1,) + shape[1:], lambda i, p: (p[1, i],) + rest)
-
-    def slot(shape):
-        rest = (0,) * (len(shape) - 4)
-        return pl.BlockSpec(
-            (1, layers, 1, 1) + shape[4:], lambda i, p: (0, 0, i // cap, i % cap) + rest
-        )
-
-    outs = [
-        (1, layers, nodes, cap, span_max, 2, feats),
-        (1, layers, nodes, cap, 2, 2, heads),
-        queries.shape,
-    ]
-    return pl.pallas_call(
-        attend_kernel,
-        grid_spec=pltpu.PrefetchScalarGridSpec(
-            num_scalar_prefetch=1,
-            grid=(nodes * cap,),
-            in_specs=[unit(s.shape) for s in stores] + [slot(queries.shape), slot(new_kv.shape)],
-            out_specs=[slot(s) for s in outs],
-        ),
-        out_shape=[jax.ShapeDtypeStruct(s, bf16) for s in outs],
+    anywhere = pl.BlockSpec(memory_space=pl.ANY)
+    vmem = pl.BlockSpec(memory_space=pltpu.VMEM)
+    smem = pl.BlockSpec(memory_space=pltpu.SMEM)
+    cache, scales, attention = pl.pallas_call(
+        place_kernel,
+        in_specs=[smem] + [vmem] * len(units),
+        out_specs=[anywhere, vmem, anywhere],
+        out_shape=[
+            jax.ShapeDtypeStruct((1, layers, nodes, cap, 2, PAGE, 2, feats), bf16),
+            jax.ShapeDtypeStruct((layers, nodes * cap, 2, 2, heads), bf16),
+            jax.ShapeDtypeStruct(queries.shape, bf16),
+        ],
+        scratch_shapes=[
+            pltpu.VMEM(units[0].shape[1:], bf16),
+            pltpu.VMEM(units[PARTS + 1].shape[1:], bf16),
+            pltpu.SemaphoreType.DMA((nodes * cap, PARTS + 1)),
+        ],
         compiler_params=pltpu.CompilerParams(vmem_limit_bytes=40 << 20),
-    )(steps, *stores, queries, new_kv)
+    )(steps, *units)
+    cache = cache.reshape(1, layers, nodes, cap, 2 * PAGE, 2, feats)
+    return cache, scales.reshape(1, layers, nodes, cap, 2, 2, heads), attention
 
 
 def slot_ranks(route):
@@ -574,9 +651,12 @@
     def direct(prompt_pages, page_scales, page_table, lengths, route, queries, new_kv):
         held = page_scales.shape[2]
         scales = page_scales.reshape(held, 2, 16, -1).transpose(2, 0, 1, 3)
-        scales = jnp.pad(scales, ((0, 0), (0, 0), (0, 0), (0, 128 - scales.shape[3])))
-        stores = exchange(steps, page_table, prompt_pages, scales)
-        return tuple(attend(steps, stores, queries, new_kv))
+        heads = scales.shape[3]
+        scales = jnp.pad(jnp.tile(scales, (1, 1, 1, 4)), ((0, 0),) * 3 + ((0, 128 - 4 * heads),))
+        own = jnp.arange(128) // heads == lax.axis_index("section")
+        scales = jnp.where(own, scales, jnp.zeros((), scales.dtype))
+        units = exchange(steps, page_table, prompt_pages, scales, queries, new_kv)
+        return tuple(place(steps, units, queries))
 
     return lax.cond(
         steps[3, 0] > 0,

time: 172 us -> 119 us (0.69)
  Pallas kernels: 164 us -> 111 us
    pallas_call x1, Pallas kernels: 56.1 us -> 4.68 us  [place(): pl.pallas_call(place_kernel, in_specs=[smem] + [vmem] * len(units), out_s...]
where the time goes in v2:
time: 119 us; the launch traced here: 118 us
  Pallas kernels  111 us (93%)
  local copies, waits for them, and re-layouts  5.44 us (5%)
  between operations  1.3 us (1%)
    pallas_call x1, Pallas kernels, exchange(): pl.pallas_call(exchange_kernel, out_shape=[jax.ShapeDtypeStruct((STORE, l...  104 us
    pallas_call x1, Pallas kernels, place(): pl.pallas_call(place_kernel, in_specs=[smem] + [vmem] * len(units), out_s...  4.68 us
    unnamed x6, local copies, waits for them, and re-layouts  3.61 us
    pallas_call x1, Pallas kernels, plan(): pl.pallas_call(plan_kernel, out_shape=jax.ShapeDtypeStruct((8, 128), jnp....  2.98 us

profile of v2, /device:TPU:2, one launch (start us, length us, event | category | flops | bytes accessed | tf_op | source)
XLA Modules:
  0.0 118.5 jit_solution(16995364965645608441)
XLA Ops:
  0.6 1.4 %copy.159.route_ref = s32[16,8]{1,0:T(8,128)} copy(s32[16,8]{0,1:T(8,128)} %param.14) | data formatting | bytes 1024 | tf_op args[4]
  2.0 1.4 %copy.160.length_ref = s32[16,8]{1,0:T(8,128)} copy(s32[16,8]{0,1:T(8,128)} %param.13) | data formatting | bytes 1024 | tf_op args[3]
  3.3 3.0 %shard_map.109 = s32[8,128]{1,0:T(8,128)S(1)} custom-call(bf16[256,16]{1,0:T(8,128)(2,1)} %constant.56.clone.table_ref, s32[16,8]{1,0:T(8,128)} %copy.159.route_ref, s32[16,8]{1,0:T(8,128)} %copy.160.length_ref), custom_call_target="tpu_custom_call" | custom-call | tf_op jit(solution)/shard_map/pallas_call | solution.py:163
  6.3 0.5 slice.21
  7.5 110.1 %conditional.1 = (bf16[1,4,16,2,32,2,384]{6,5,4,3,2,1,0:T(2,128)(2,1)}, bf16[1,4,16,2,8,384]{5,4,3,2,1,0:T(8,128)(2,1)S(1)}, bf16[1,4,16,2,2,2,3]{2,5,6,4,3,1,0:T(2,128)(2,1)S(1)}) conditional(s32[]{:T(128)} %bitcast.41, (s32[16,8]{0,1:T(8,128)}, bf16[1,1,4,16,2,6144]{5,4,3,2,1,0:T(2,128)(2,1)}, s32[1,16]{1,0:T(1,128)}, ...), branch_computations={%region_0.10_spmd, %region_10.11_spmd} | conditional | flops 68673144 | bytes 158821696 | solution.py:661
  7.7 0.8 reshape.195
  8.5 0.1 copy.130
  8.7 0.1 copy.131
  8.9 103.7 %branch_1_fun.2 = (bf16[56,4,2,4,2,384]{5,4,3,2,1,0:T(2,128)(2,1)S(1)}, bf16[56,4,2,4,2,384]{5,4,3,2,1,0:T(2,128)(2,1)S(1)}, bf16[56,4,2,4,2,384]{5,4,3,2,1,0:T(...) custom-call(s32[8,128]{1,0:T(8,128)S(1)} %get-tuple-element.33.plan_, ...), custom_call_target="tpu_custom_call" | custom-call | bytes 20971520 | tf_op jit(solution)/shard_map/cond/branch_1_fun/pallas_call | solution.py:401
  112.6 4.7 %branch_1_fun.3 = (bf16[1,4,16,2,2,16,2,384]{7,6,5,4,3,2,1,0:T(2,128)(2,1)}, bf16[4,32,2,2,3]{4,3,2,1,0:T(2,128)(2,1)S(1)}, bf16[1,4,16,2,8,384]{5,4,3,2,1,0:T(8,128)(2,1)S(1)}) custom-call(s32[8,128]{1,0:T(8,128)S(1)} %get-tuple-element.33.plan_ref, bf16[56,4,2,4,2,384]{5,4,3,2,1,0:T(2,128)(2,1)S(1)} %get-tuple-element.39.refs_0_, ...), custom_call_target="tpu_custom_call" | custom-call | tf_op jit(solution)/shard_map/cond/branch_1_fun/pallas_call | solution.py:474
  117.3 0.3 copy.170
  117.6 0.0 copy-start.9
  117.6 0.0 copy-start.11
  117.6 0.6 copy-done.9
  118.2 0.3 copy-done.11
  (3 shorter events, 0.1 us)
Async XLA Ops:
  117.6 0.6 copy-start.9
  117.6 0.9 copy-start.11
